TPU v7x, 32 devices: a whole 2x2x4 slice. The times are simulated.
32 devices in a mesh: row: 8 (over z, x), col: 4 (over y, core).
Axes of the slice: x: 2, y: 2, z: 4, core: 2. Of those that a mesh axis runs over, the one named last changes fastest.
Arguments:
- traces: bfloat16 [4096, 1024], P(('row', 'col'))
- alive: int32 [4096], P(('row', 'col')), may hold values 0 or 1
- pair_list: int32 [128, 2], P(('row', 'col')), may hold values from -1 to 31, as said below
Outputs:
- correlations: bfloat16 [128, 128, 65, 128], P(('row', 'col'))
Inputs may be any that keep to these rules, and one draw needn't show every extreme that they name: `pair_list`: slots p * 4 to (p + 1) * 4 - 1 belong to flat device p = r * 4 + c (r its row index, c its col index); they hold 1 to 4 live pairs first and then (-1, -1) pairs; in every draw some device has all 4 slots live. A live pair (a, b) of that device has a // 4 == r, b % 4 == c and b >= a.
All inputs are finite; a program needn't handle non-finite values. No bound on the sum of `alive` on one device may be relied on, other than what follows from the above.
Results may differ from a plain program's by a relative error of at most 0.0042.
Values may be sent and summed in bfloat16 or wider, within the bound.
A program may use at most 128 MiB of HBM per device.

v0:
```python
import jax
import jax.numpy as jnp
from jax import lax
from jax.sharding import PartitionSpec as P

LAGS = 65


def whiten(traces, alive):
    samples = traces.astype(jnp.float32)
    centered = samples - jnp.mean(samples, axis=1, keepdims=True)
    power = jnp.mean(centered * centered, axis=1, keepdims=True)
    factor = alive.astype(jnp.float32)[:, None] / jnp.sqrt(power + 1e-05)
    return (centered * factor).astype(jnp.bfloat16)


def correlate(left_block, right_block):
    length = left_block.shape[1]
    width = left_block.shape[0]
    reach = (LAGS - 1) // 2
    padded = jnp.pad(right_block, ((0, 0), (reach, reach)))
    shifted = jnp.stack([padded[:, offset : offset + length] for offset in range(LAGS)], axis=0)
    shifted = shifted.reshape(LAGS * width, length)
    summed = lax.dot_general(
        left_block, shifted, (((1,), (1,)), ((), ())), preferred_element_type=jnp.float32
    )
    return (summed * (1.0 / length)).reshape(width, LAGS, width).astype(jnp.bfloat16)


def shards(traces, alive, pair_list):
    whitened = whiten(traces, alive)
    block = whitened.shape[0]
    slots = pair_list.shape[0]
    across = lax.axis_size("col")
    row_panel = lax.all_gather(whitened, "col", axis=0, tiled=True)
    row_first = lax.axis_index("row") * across
    row_place = jnp.maximum(pair_list[:, 0] - row_first, 0)
    col_place = jnp.maximum(pair_list[:, 1], 0) // across
    living = jnp.sum((pair_list[:, 0] >= 0).astype(jnp.int32))
    buffer = jnp.zeros((slots, block, LAGS, block), jnp.bfloat16)

    def left_of(slot):
        return lax.dynamic_slice_in_dim(row_panel, row_place[slot] * block, block, 0)

    col_panel = lax.all_gather(whitened, "row", axis=0, tiled=True)

    def one_slot(slot, result):
        right_block = lax.dynamic_slice_in_dim(col_panel, col_place[slot] * block, block, 0)
        return lax.dynamic_update_index_in_dim(
            result, correlate(left_of(slot), right_block), slot, 0
        )

    correlations = lax.fori_loop(0, living, one_slot, buffer)
    return correlations


def solution(mesh):
    in_specs = (P(("row", "col"), None), P(("row", "col")), P(("row", "col"), None))
    out_specs = P(("row", "col"), None, None, None)
    return jax.shard_map(shards, mesh=mesh, in_specs=in_specs, out_specs=out_specs, check_vma=False)
```

profile of v0, /device:TPU:0, one launch (start us, length us, event | category | flops | bytes accessed | tf_op | source)
XLA Modules:
  0.0 251.1 jit_solution(16588844642128723072)
XLA Ops:
  9.4 1.9 fusion.6
  14.1 16.8 %all-gather.3.cloned.1.call-done = bf16[512,1024]{1,0:T(8,128)(2,1)} async-done(((bf16[128,1024]{1,0:T(8,128)(2,1)}), bf16[512,1024]{1,0:T(8,128)(2,1)}) %all-gather.3.cloned.1.call-update) | async-done | bytes 1048592 | tf_op jit(solution)/shard_map/all_gather | solution.py:35
  30.9 51.4 %all-gather.5.cloned.1.call-done = bf16[1024,1024]{1,0:T(8,128)(2,1)} async-done(((bf16[128,1024]{1,0:T(8,128)(2,1)}), bf16[1024,1024]{1,0:T(8,128)(2,1)}) %all-gather.5.cloned.1.call-update) | async-done | bytes 2097168 | tf_op jit(solution)/shard_map/all_gather | solution.py:45
  82.4 5.6 %broadcast_in_dim.3.clone = bf16[4,128,65,128]{3,1,2,0:T(8,128)(2,1)} broadcast(bf16[]{:T(256)} %constant.71.clone.1), dimensions={} | broadcast | bytes 8519682 | tf_op jit(solution)/shard_map/broadcast_in_dim | solution.py:40
  88.0 156.2 %while.12 = (s32[]{:T(128)}, bf16[4,128,65,128]{3,1,2,0:T(8,128)(2,1)}, s32[]{:T(128)}, s32[4]{0:T(128)S(1)}, bf16[512,1024]{1,0:T(8,128)(2,1)}, /*index=5*/s32[...) while((s32[]{:T(128)}, ...), condition=%wide.region_4.5_spmd, body=%wide.region_3.4_spmd.sunk | while | flops 2183168000 | bytes 134971696 | solution.py:53
  100.9 5.8 %copy-done = bf16[65,128,1024]{2,1,0:T(8,128)(2,1)} copy-done((bf16[65,128,1024]{2,1,0:T(8,128)(2,1)}, bf16[65,128,1024]{2,1,0:T(8,128)(2,1)S(1)}, u32[]{:S(2)}) %copy-start) | copy-done | bytes 17039384 | tf_op jit(solution)/shard_map/while
  108.1 11.5 %fusion.14 = bf16[128,8320]{1,0:T(8,128)(2,1)S(1)} fusion(bf16[8320,1024]{1,0:T(8,128)(2,1)} %bitcast.281, bf16[512,1024]{1,0:T(8,128)(2,1)} %get-tuple-element.188, s32[]{:T(128)S(6)} %select_n.33), kind=kOutput, calls=%fused_computation.1.clone.1 | convolution fusion | flops 2183168000 | bytes 19431428 | tf_op jit(solution)/shard_map/while/body/dot_general | solution.py:24
  119.6 2.4 copy.11
  122.1 3.3 %copy.12 = bf16[1,128,65,128]{3,1,2,0:T(8,128)(2,1)S(1)} copy(bf16[1,128,65,128]{1,3,2,0:T(8,128)(2,1)} %bitcast.282) | data formatting | bytes 4259840 | tf_op jit(solution)/shard_map/while/body/jit(dynamic_update_index_in_dim)/dynamic_update_slice | solution.py:49
  125.4 1.5 constant_dynamic-update-slice_fusion.2
  139.8 5.8 %copy-done = bf16[65,128,1024]{2,1,0:T(8,128)(2,1)} copy-done((bf16[65,128,1024]{2,1,0:T(8,128)(2,1)}, bf16[65,128,1024]{2,1,0:T(8,128)(2,1)S(1)}, u32[]{:S(2)}) %copy-start) | copy-done | bytes 17039384 | tf_op jit(solution)/shard_map/while
  147.0 11.5 %fusion.14 = bf16[128,8320]{1,0:T(8,128)(2,1)S(1)} fusion(bf16[8320,1024]{1,0:T(8,128)(2,1)} %bitcast.281, bf16[512,1024]{1,0:T(8,128)(2,1)} %get-tuple-element.188, s32[]{:T(128)S(6)} %select_n.33), kind=kOutput, calls=%fused_computation.1.clone.1 | convolution fusion | flops 2183168000 | bytes 19431428 | tf_op jit(solution)/shard_map/while/body/dot_general | solution.py:24
  158.6 2.4 copy.11
  161.0 3.3 %copy.12 = bf16[1,128,65,128]{3,1,2,0:T(8,128)(2,1)S(1)} copy(bf16[1,128,65,128]{1,3,2,0:T(8,128)(2,1)} %bitcast.282) | data formatting | bytes 4259840 | tf_op jit(solution)/shard_map/while/body/jit(dynamic_update_index_in_dim)/dynamic_update_slice | solution.py:49
  164.3 1.5 constant_dynamic-update-slice_fusion.2
  178.8 5.8 %copy-done = bf16[65,128,1024]{2,1,0:T(8,128)(2,1)} copy-done((bf16[65,128,1024]{2,1,0:T(8,128)(2,1)}, bf16[65,128,1024]{2,1,0:T(8,128)(2,1)S(1)}, u32[]{:S(2)}) %copy-start) | copy-done | bytes 17039384 | tf_op jit(solution)/shard_map/while
  185.9 11.5 %fusion.14 = bf16[128,8320]{1,0:T(8,128)(2,1)S(1)} fusion(bf16[8320,1024]{1,0:T(8,128)(2,1)} %bitcast.281, bf16[512,1024]{1,0:T(8,128)(2,1)} %get-tuple-element.188, s32[]{:T(128)S(6)} %select_n.33), kind=kOutput, calls=%fused_computation.1.clone.1 | convolution fusion | flops 2183168000 | bytes 19431428 | tf_op jit(solution)/shard_map/while/body/dot_general | solution.py:24
  197.5 2.4 copy.11
  199.9 3.3 %copy.12 = bf16[1,128,65,128]{3,1,2,0:T(8,128)(2,1)S(1)} copy(bf16[1,128,65,128]{1,3,2,0:T(8,128)(2,1)} %bitcast.282) | data formatting | bytes 4259840 | tf_op jit(solution)/shard_map/while/body/jit(dynamic_update_index_in_dim)/dynamic_update_slice | solution.py:49
  203.2 1.5 constant_dynamic-update-slice_fusion.2
  217.7 5.8 %copy-done = bf16[65,128,1024]{2,1,0:T(8,128)(2,1)} copy-done((bf16[65,128,1024]{2,1,0:T(8,128)(2,1)}, bf16[65,128,1024]{2,1,0:T(8,128)(2,1)S(1)}, u32[]{:S(2)}) %copy-start) | copy-done | bytes 17039384 | tf_op jit(solution)/shard_map/while
  224.9 11.5 %fusion.14 = bf16[128,8320]{1,0:T(8,128)(2,1)S(1)} fusion(bf16[8320,1024]{1,0:T(8,128)(2,1)} %bitcast.281, bf16[512,1024]{1,0:T(8,128)(2,1)} %get-tuple-element.188, s32[]{:T(128)S(6)} %select_n.33), kind=kOutput, calls=%fused_computation.1.clone.1 | convolution fusion | flops 2183168000 | bytes 19431428 | tf_op jit(solution)/shard_map/while/body/dot_general | solution.py:24
  236.4 2.4 copy.11
  238.9 3.3 %copy.12 = bf16[1,128,65,128]{3,1,2,0:T(8,128)(2,1)S(1)} copy(bf16[1,128,65,128]{1,3,2,0:T(8,128)(2,1)} %bitcast.282) | data formatting | bytes 4259840 | tf_op jit(solution)/shard_map/while/body/jit(dynamic_update_index_in_dim)/dynamic_update_slice | solution.py:49
  (287 shorter events, 55.2 us)
Async XLA Ops:
  6.5 24.4 %all-gather.3.cloned.1.call-start = ((), (), s32[]{:S(2)}) async-start(), calls=%async_computation | async-start | bytes 1310720 | tf_op jit(solution)/shard_map/all_gather | solution.py:35
  11.3 71.0 %all-gather.5.cloned.1.call-start = ((), (), s32[]{:S(2)}) async-start(), calls=%async_computation.1 | async-start | bytes 2359296 | tf_op jit(solution)/shard_map/all_gather | solution.py:45
  100.9 5.8 %copy-start = (bf16[65,128,1024]{2,1,0:T(8,128)(2,1)}, bf16[65,128,1024]{2,1,0:T(8,128)(2,1)S(1)}, u32[]{:S(2)}) copy-start(bf16[65,128,1024]{2,1,0:T(8,128)(2,1)S(1)} %bitcast_dynamic-update-slice_fusion.194) | copy-start | bytes 51118084 | tf_op jit(solution)/shard_map/while
  139.8 5.8 %copy-start = (bf16[65,128,1024]{2,1,0:T(8,128)(2,1)}, bf16[65,128,1024]{2,1,0:T(8,128)(2,1)S(1)}, u32[]{:S(2)}) copy-start(bf16[65,128,1024]{2,1,0:T(8,128)(2,1)S(1)} %bitcast_dynamic-update-slice_fusion.194) | copy-start | bytes 51118084 | tf_op jit(solution)/shard_map/while
  178.7 5.8 %copy-start = (bf16[65,128,1024]{2,1,0:T(8,128)(2,1)}, bf16[65,128,1024]{2,1,0:T(8,128)(2,1)S(1)}, u32[]{:S(2)}) copy-start(bf16[65,128,1024]{2,1,0:T(8,128)(2,1)S(1)} %bitcast_dynamic-update-slice_fusion.194) | copy-start | bytes 51118084 | tf_op jit(solution)/shard_map/while
  217.7 5.8 %copy-start = (bf16[65,128,1024]{2,1,0:T(8,128)(2,1)}, bf16[65,128,1024]{2,1,0:T(8,128)(2,1)S(1)}, u32[]{:S(2)}) copy-start(bf16[65,128,1024]{2,1,0:T(8,128)(2,1)S(1)} %bitcast_dynamic-update-slice_fusion.194) | copy-start | bytes 51118084 | tf_op jit(solution)/shard_map/while
Sparse Core Ops, SparseCore 0:
  11.5 19.4 all-gather.2
  33.0 49.2 all-gather.4
where the time goes:
time: 252 us; the launch traced here: 251 us
  local copies, waits for them, and re-layouts  106 us (42%)
  waiting for transfers between devices  69 us (27%)
  matrix products  46.1 us (18%)
  between operations  13.4 us (5%)
  loops' own time  9.85 us (4%)
  other arithmetic  6.78 us (3%)
    while x264, local copies, waits for them, and re-layouts  61.9 us
    all_gather x1, waiting for transfers between devices, shards(): col_panel = lax.all_gather(whitened, 'row', axis=0, tiled=True)  51.4 us
    dot_general x4, matrix products, correlate(): lax.dot_general(left_block, shifted, (((1,), (1,)), ((), ())), preferred_...  46.1 us
    dynamic_update_slice x8, local copies, waits for them, and re-layouts, one_slot(): lax.dynamic_update_index_in_dim(result, correlate(left_of(slot), right_bl...  19.1 us
    all_gather x1, waiting for transfers between devices, shards(): row_panel = lax.all_gather(whitened, 'col', axis=0, tiled=True)  16.8 us
    another operation x1, loops' own time, shards(): correlations = lax.fori_loop(0, living, one_slot, buffer)  9.85 us
    convert_element_type x4, local copies, waits for them, and re-layouts, correlate(): (summed * (1.0 / length)).reshape(width, LAGS, width).astype(jnp.bfloat16)  9.8 us
    broadcast_in_dim x1, local copies, waits for them, and re-layouts, shards(): buffer = jnp.zeros((slots, block, LAGS, block), jnp.bfloat16)  5.6 us
  transfers between devices with their start and end apart: 2, of which 2 were waited for; matrix products, arithmetic and copies ran while one was open for 1% of the time, Pallas kernels for 0%

commit v1 on v0

v1 whole, which is shorter than its diff:
```python
import functools

import jax
import jax.numpy as jnp
from jax import lax
from jax.experimental import pallas as pl
from jax.experimental.pallas import tpu as pltpu
from jax.sharding import PartitionSpec as P

LAGS = 65
REACH = (LAGS - 1) // 2
STEP = 8
MESH = pl.DeviceIdType.MESH


def whiten(traces, alive):
    samples = traces.astype(jnp.float32)
    centered = samples - jnp.mean(samples, axis=1, keepdims=True)
    power = jnp.mean(centered * centered, axis=1, keepdims=True)
    factor = alive.astype(jnp.float32) / jnp.sqrt(power + 1e-05)
    return (centered * factor).astype(jnp.bfloat16)


def gather_kernel(grid, traces_ref, alive_ref, row_ref, col_ref, own, z_send, x_send, y_send,
                  col_recv, row_recv, local_sem):
    deep, wide, across = grid
    row, col = lax.axis_index("row"), lax.axis_index("col")
    z, x = row // wide, row % wide

    def at(r, c):
        return (r, c)

    barrier = pltpu.get_barrier_semaphore()

    def greet(r, c):
        pl.semaphore_signal(barrier, inc=1, device_id=at(r, c), device_id_type=MESH)

    pl.when(z > 0)(lambda: greet(row - wide, col))
    pl.when(z < deep - 1)(lambda: greet(row + wide, col))
    for step in range(1, wide):
        greet(z * wide + (x + step) % wide, col)
    for step in range(1, across):
        greet(row, (col + step) % across)

    alive = jnp.broadcast_to(alive_ref[...].astype(jnp.float32), (own.shape[0], own.shape[0]))
    own[...] = whiten(traces_ref[...], alive.T[:, :1])

    peers = wide - 1 + across - 1 + (z > 0).astype(jnp.int32) + (z < deep - 1).astype(jnp.int32)
    pl.semaphore_wait(barrier, peers)

    def down(source, block):
        return pltpu.make_async_remote_copy(
            src_ref=source, dst_ref=col_ref.at[block], send_sem=z_send.at[block // wide],
            recv_sem=col_recv.at[block], device_id=at(row - wide, col), device_id_type=MESH)

    def side(source, block, step):
        return pltpu.make_async_remote_copy(
            src_ref=source, dst_ref=col_ref.at[block], send_sem=x_send.at[block // wide, step],
            recv_sem=col_recv.at[block], device_id=at(z * wide + (x + step) % wide, col),
            device_id_type=MESH)

    def along(step):
        return pltpu.make_async_remote_copy(
            src_ref=own, dst_ref=row_ref.at[col], send_sem=y_send.at[step],
            recv_sem=row_recv.at[col], device_id=at(row, (col + step) % across),
            device_id_type=MESH)

    def arrived(ref, place, sem):
        pltpu.make_async_copy(ref.at[place], ref.at[place], sem.at[place]).wait()

    pl.when(z > 0)(lambda: down(own, row).start())
    for step in range(1, wide):
        pl.when((x + step) % wide < x)(lambda step=step: side(own, row, step).start())
    for step in range(1, across):
        along(step).start()
    keep_col = pltpu.make_async_copy(own, col_ref.at[row], local_sem.at[0])
    keep_row = pltpu.make_async_copy(own, row_ref.at[col], local_sem.at[1])
    keep_col.start()
    keep_row.start()

    for hop in range(1, deep):
        @pl.when(z + hop < deep)
        def _(hop=hop):
            block = row + hop * wide
            arrived(col_ref, block, col_recv)
            pl.when(z > 0)(lambda: down(col_ref.at[block], block).start())
            for step in range(1, wide):
                side(col_ref.at[block], block, step).start()

    for step in range(1, wide):
        other = (x + step) % wide
        pl.when(other > x)(lambda other=other: arrived(col_ref, z * wide + other, col_recv))
        for hop in range(1, deep):
            pl.when(z + hop < deep)(
                lambda other=other, hop=hop: arrived(col_ref, (z + hop) * wide + other, col_recv))
    for step in range(1, across):
        arrived(row_ref, (col + step) % across, row_recv)

    keep_col.wait()
    keep_row.wait()
    pl.when(z > 0)(lambda: down(own, row).wait_send())
    for step in range(1, wide):
        pl.when((x + step) % wide < x)(lambda step=step: side(own, row, step).wait_send())
    for step in range(1, across):
        along(step).wait_send()
    for hop in range(1, deep):
        @pl.when(z + hop < deep)
        def _(hop=hop):
            block = row + hop * wide
            pl.when(z > 0)(lambda: down(col_ref.at[block], block).wait_send())
            for step in range(1, wide):
                side(col_ref.at[block], block, step).wait_send()


def gather(traces, alive):
    block, length = traces.shape
    rows, across = lax.axis_size("row"), lax.axis_size("col")
    deep = 4 if rows % 4 == 0 else 1
    wide = rows // deep
    return pl.pallas_call(
        functools.partial(gather_kernel, (deep, wide, across)),
        out_shape=(
            jax.ShapeDtypeStruct((across, block, length), jnp.bfloat16),
            jax.ShapeDtypeStruct((rows, block, length), jnp.bfloat16),
        ),
        in_specs=[pl.BlockSpec(memory_space=pltpu.VMEM)] * 2,
        out_specs=(pl.BlockSpec(memory_space=pl.ANY), pl.BlockSpec(memory_space=pl.ANY)),
        scratch_shapes=[
            pltpu.VMEM((block, length), jnp.bfloat16),
            pltpu.SemaphoreType.DMA((deep,)),
            pltpu.SemaphoreType.DMA((deep, wide)),
            pltpu.SemaphoreType.DMA((across,)),
            pltpu.SemaphoreType.DMA((rows,)),
            pltpu.SemaphoreType.DMA((across,)),
            pltpu.SemaphoreType.DMA((2,)),
        ],
        compiler_params=pltpu.CompilerParams(
            collective_id=0, has_side_effects=True, vmem_limit_bytes=32 * 1024 * 1024),
        name="gather",
    )(traces, alive.reshape(1, block))


def shifted(array, amount):
    width, length = array.shape
    if amount == 0:
        return array
    empty = jnp.zeros((width, abs(amount)), array.dtype)
    if amount > 0:
        return jnp.concatenate([empty, array[:, : length - amount]], axis=1)
    return jnp.concatenate([array[:, -amount:], empty], axis=1)


def pair_kernel(row_place, col_place, live, left_ref, right_ref, out_ref, lefts, rights):
    slot = pl.program_id(0)
    width, length = left_ref.shape[1:]
    scale = 1.0 / length

    def product(a, b):
        return lax.dot_general(
            a, b, (((1,), (1,)), ((), ())), preferred_element_type=jnp.float32)

    @pl.when(live[slot] == 0)
    def _():
        out_ref[...] = jnp.zeros_like(out_ref)

    @pl.when(live[slot] != 0)
    def _():
        left, right = left_ref[0], right_ref[0]
        out_ref[0, REACH] = (product(left, right) * scale).astype(jnp.bfloat16)
        for sign in (1, -1):
            for shift in range(STEP):
                lefts[shift * width : (shift + 1) * width, :] = shifted(left, sign * (shift + 1))
            for pair in range(REACH // STEP // 2):
                for half in range(2):
                    rights[half * width : (half + 1) * width, :] = shifted(
                        right, -sign * STEP * (2 * pair + half))
                summed = product(lefts[...], rights[...])
                scaled = (summed * scale).astype(jnp.bfloat16)
                for half in range(2):
                    for shift in range(STEP):
                        lag = REACH + sign * (STEP * (2 * pair + half) + shift + 1)
                        out_ref[0, lag] = scaled[
                            shift * width : (shift + 1) * width, half * width : (half + 1) * width]


def correlate(row_place, col_place, live, row_panel, col_panel):
    slots = live.shape[0]
    _, width, length = row_panel.shape
    return pl.pallas_call(
        pair_kernel,
        grid_spec=pltpu.PrefetchScalarGridSpec(
            num_scalar_prefetch=3,
            grid=(slots,),
            in_specs=[
                pl.BlockSpec((1, width, length), lambda s, r, c, l: (r[s], 0, 0)),
                pl.BlockSpec((1, width, length), lambda s, r, c, l: (c[s], 0, 0)),
            ],
            out_specs=pl.BlockSpec((1, LAGS, width, width), lambda s, r, c, l: (s, 0, 0, 0)),
            scratch_shapes=[
                pltpu.VMEM((STEP * width, length), jnp.bfloat16),
                pltpu.VMEM((2 * width, length), jnp.bfloat16),
            ],
        ),
        out_shape=jax.ShapeDtypeStruct((slots, LAGS, width, width), jnp.bfloat16),
        compiler_params=pltpu.CompilerParams(vmem_limit_bytes=48 * 1024 * 1024),
        name="pairs",
    )(row_place, col_place, live, row_panel, col_panel)


def shards(traces, alive, pair_list):
    across = lax.axis_size("col")
    row_first = lax.axis_index("row") * across
    row_place = jnp.clip(pair_list[:, 0] - row_first, 0, across - 1)
    col_place = jnp.maximum(pair_list[:, 1], 0) // across
    live = (pair_list[:, 0] >= 0).astype(jnp.int32)
    row_panel, col_panel = gather(traces, alive)
    lagged = correlate(row_place, col_place, live, row_panel, col_panel)
    return jnp.transpose(lagged, (0, 2, 1, 3))


def solution(mesh):
    in_specs = (P(("row", "col"), None), P(("row", "col")), P(("row", "col"), None))
    out_specs = P(("row", "col"), None, None, None)
    return jax.shard_map(shards, mesh=mesh, in_specs=in_specs, out_specs=out_specs, check_vma=False)
```

time: 252 us -> 48.3 us (0.19)
  local copies, waits for them, and re-layouts: 106 us -> 1.6 us
  waiting for transfers between devices: 69 us -> 0 us
  matrix products: 46.1 us -> 0 us
  Pallas kernels: 0 us -> 44.4 us
  between operations: 13.4 us -> 0.01 us
  loops' own time: 9.85 us -> 0 us
  other arithmetic: 6.78 us -> 2.05 us
    all_gather x2 -> x0, waiting for transfers between devices: 68.3 us -> none  [the longest x1 51.4 us: shards(): col_panel = lax.all_gather(whitened, 'row', axis=0, tiled=True)]
    while x264 -> x0, local copies, waits for them, and re-layouts: 61.9 us -> none
    dot_general x4 -> x0, matrix products: 46.1 us -> none  [correlate(): lax.dot_general(left_block, shifted, (((1,), (1,)), ((), ())), preferred_...]
    pallas_call x0 -> x2, Pallas kernels: none -> 44.4 us  [the longest x1 32.6 us: gather(): pl.pallas_call(functools.partial(gather_kernel, (deep, wide, across)), ou...]
    dynamic_update_slice x8 -> x0, local copies, waits for them, and re-layouts: 19.1 us -> none  [one_slot(): lax.dynamic_update_index_in_dim(result, correlate(left_of(slot), right_bl...]
    another operation x1 -> x0, loops' own time: 9.85 us -> none  [shards(): correlations = lax.fori_loop(0, living, one_slot, buffer)]
    convert_element_type x4 -> x0, local copies, waits for them, and re-layouts: 9.8 us -> none  [correlate(): (summed * (1.0 / length)).reshape(width, LAGS, width).astype(jnp.bfloat16)]
    dynamic_slice x12 -> x0, local copies, waits for them, and re-layouts: 8.87 us -> none  [the longest x4 3.89 us: one_slot(): lax.dynamic_slice_in_dim(col_panel, col_place[slot] * block, block, 0)]
  transfers between devices with their start and end apart: 2 -> 0, of which waited for: 2 -> 0; matrix products, arithmetic and copies ran while one was open for 1% -> 0% of each run, Pallas kernels for 0% -> 0%
where the time goes in v1:
time: 48.3 us; the launch traced here: 48.1 us
  Pallas kernels  44.4 us (92%)
  other arithmetic  2.05 us (4%)
  local copies, waits for them, and re-layouts  1.6 us (3%)
    pallas_call x1, Pallas kernels, gather(): pl.pallas_call(functools.partial(gather_kernel, (deep, wide, across)), ou...  32.6 us
    pallas_call x1, Pallas kernels, correlate(): pl.pallas_call(pair_kernel, grid_spec=pltpu.PrefetchScalarGridSpec(num_sc...  11.8 us
    unnamed x4, local copies, waits for them, and re-layouts  1.6 us

profile of v1, /device:TPU:0, one launch (start us, length us, event | category | flops | bytes accessed | tf_op | source)
XLA Modules:
  0.0 48.1 jit_solution(2840486180012867941)
XLA Ops:
  0.0 0.7 %clamp_bitcast_fusion.row_place = s32[4]{0:T(128)S(1)} fusion(s32[4,2]{0,1:T(2,128)} %param.5, s32[]{:T(128)S(6)} %mul.3), kind=kLoop, calls=%fused_computation.3 | loop fusion | flops 8 | bytes 36 | tf_op jit(solution)/shard_map/jit(clip)/min | solution.py:213
  0.7 0.7 %fusion.live = s32[4]{0:T(128)S(1)} fusion(s32[4,2]{0,1:T(2,128)} %param.5), kind=kLoop, calls=%fused_computation.2 | loop fusion | flops 8 | bytes 32 | tf_op jit(solution)/shard_map/convert_element_type | solution.py:215
  1.4 0.7 %bitcast_select_fusion.col_place = s32[4]{0:T(128)S(1)} fusion(s32[4,2]{0,1:T(2,128)} %param.5), kind=kLoop, calls=%fused_computation | loop fusion | flops 36 | bytes 32 | tf_op jit(solution)/shard_map/jit(floor_divide)/jit(_where)/select_n | solution.py:214
  2.1 0.0 copy-start
  2.1 0.9 %copy-done = bf16[128,1024]{1,0:T(8,128)(2,1)S(1)} copy-done((bf16[128,1024]{1,0:T(8,128)(2,1)S(1)}, bf16[128,1024]{1,0:T(8,128)(2,1)}, u32[]{:S(2)}) %copy-start) | copy-done | bytes 262168
  3.0 0.0 copy-start.1
  3.0 0.7 %copy-done.1 = s32[128]{0:T(128)S(1)} copy-done((s32[128]{0:T(128)S(1)}, s32[128]{0:T(128)}, u32[]{:S(2)}) %copy-start.1) | copy-done | bytes 536
  3.7 32.6 %gather.1 = (bf16[4,128,1024]{2,1,0:T(8,128)(2,1)S(1)}, bf16[8,128,1024]{2,1,0:T(8,128)(2,1)S(1)}) custom-call(bf16[128,1024]{1,0:T(8,128)(2,1)S(1)} %copy-done, s32[1,128]{1,0:T(1,128)S(1)} %bitcast.10), custom_call_target="tpu_custom_call" | custom-call | tf_op jit(solution)/shard_map/gather/pallas_call | solution.py:120
  36.3 11.8 %pairs.1 = bf16[4,65,128,128]{3,2,1,0:T(8,128)(2,1)} custom-call(s32[4]{0:T(128)S(1)} %clamp_bitcast_fusion.row_place, s32[4]{0:T(128)S(1)} %bitcast_select_fusion.col_place, s32[4]{0:T(128)S(1)} %fusion.live, bf16[4,128,1024]{2,1,0:T(8,128)(2,1)S(1)} %get-tuple-element.7.left_ref, bf16[8,128,1024]{2,1,0:T(8,128)(2,1)S(1)} %get-tuple-element.8.right_ref), custom_call_target="tpu_custom_call" | custom-call | tf_op jit(solution)/shard_map/pairs/pallas_call | solution.py:189
Async XLA Ops:
  2.1 0.9 %copy-start = (bf16[128,1024]{1,0:T(8,128)(2,1)S(1)}, bf16[128,1024]{1,0:T(8,128)(2,1)}, u32[]{:S(2)}) copy-start(bf16[128,1024]{1,0:T(8,128)(2,1)} %traces_ref.1) | copy-start | bytes 786436
  3.0 0.7 %copy-start.1 = (s32[128]{0:T(128)S(1)}, s32[128]{0:T(128)}, u32[]{:S(2)}) copy-start(s32[128]{0:T(128)} %param.4) | copy-start | bytes 1540

commit v2 on v0

v2 whole, which is shorter than its diff:
```python
import functools

import jax
import jax.numpy as jnp
from jax import lax
from jax.experimental import pallas as pl
from jax.experimental.pallas import tpu as pltpu
from jax.sharding import PartitionSpec as P

LAGS = 65
REACH = (LAGS - 1) // 2
STEP = 8
PARTS = 4
MESH = pl.DeviceIdType.MESH


def whiten(traces, alive):
    samples = traces.astype(jnp.float32)
    centered = samples - jnp.mean(samples, axis=1, keepdims=True)
    power = jnp.mean(centered * centered, axis=1, keepdims=True)
    factor = alive.astype(jnp.float32) / jnp.sqrt(power + 1e-05)
    return (centered * factor).astype(jnp.bfloat16)


def in_hbm(array):
    return pltpu.with_memory_space_constraint(array, pltpu.HBM)


def gather_kernel(grid, traces_hbm, alive_hbm, row_ref, col_ref, traces_ref, alive_ref, own,
                  z_send, x_send, y_send, relay_send, col_recv, row_recv, local_sem, load_sem):
    deep, wide, across, parts = grid
    row, col = lax.axis_index("row"), lax.axis_index("col")
    z, x = row // wide, row % wide
    part = own.shape[0] // parts
    relayed = parts // 2 if wide == 2 and deep > 1 else 0
    relays = (z == 1) & (x == 0)
    spared = (z == 0) & (x == 1)

    load_alive = pltpu.make_async_copy(alive_hbm, alive_ref, load_sem.at[parts])
    load_alive.start()

    def piece(h):
        return pl.ds(h * part, part)

    def load(h):
        return pltpu.make_async_copy(
            traces_hbm.at[piece(h)], traces_ref.at[piece(h)], load_sem.at[h])

    for h in range(parts):
        load(h).start()

    barrier = pltpu.get_barrier_semaphore()

    def greet(r, c):
        pl.semaphore_signal(barrier, inc=1, device_id=(r, c), device_id_type=MESH)

    pl.when(z > 0)(lambda: greet(row - wide, col))
    pl.when(z < deep - 1)(lambda: greet(row + wide, col))
    for step in range(1, wide):
        greet(z * wide + (x + step) % wide, col)
    for step in range(1, across):
        greet(row, (col + step) % across)

    def down(source, block, h, sem):
        return pltpu.make_async_remote_copy(
            src_ref=source.at[piece(h)], dst_ref=col_ref.at[block, piece(h)], send_sem=sem,
            recv_sem=col_recv.at[block, h], device_id=(row - wide, col), device_id_type=MESH)

    def side(source, block, step, h):
        return pltpu.make_async_remote_copy(
            src_ref=source.at[piece(h)], dst_ref=col_ref.at[block, piece(h)],
            send_sem=x_send.at[block // wide, step, h], recv_sem=col_recv.at[block, h],
            device_id=(z * wide + (x + step) % wide, col), device_id_type=MESH)

    def along(step, h):
        return pltpu.make_async_remote_copy(
            src_ref=own.at[piece(h)], dst_ref=row_ref.at[col, piece(h)],
            send_sem=y_send.at[step, h], recv_sem=row_recv.at[col, h],
            device_id=(row, (col + step) % across), device_id_type=MESH)

    def arrived(ref, place, h, sem):
        spot = ref.at[place, piece(h)]
        pltpu.make_async_copy(spot, spot, sem.at[place, h]).wait()

    def send_own(h, verb):
        pl.when(z > 0)(lambda: verb(down(own, row, h, z_send.at[z, h])))
        for step in range(1, wide):
            pl.when((x + step) % wide < x)(lambda step=step: verb(side(own, row, step, h)))
        for step in range(1, across):
            verb(along(step, h))

    def send_on(hop, h, verb):
        block = row + hop * wide
        pl.when(z > 0)(lambda: verb(down(col_ref.at[block], block, h, z_send.at[z + hop, h])))
        for step in range(1, wide):
            go = lambda step=step: verb(side(col_ref.at[block], block, step, h))
            if hop == 1 and h < relayed:
                pl.when(jnp.logical_not(spared))(go)
            else:
                go()

    def relay(h, verb):
        block = row + 1
        verb(down(col_ref.at[block], block, h, relay_send.at[h]))

    start = lambda copy: copy.start()
    sent = lambda copy: copy.wait_send()

    load_alive.wait()
    alive = jnp.broadcast_to(alive_ref[...].astype(jnp.float32), (own.shape[0], own.shape[0]))
    alive = alive.T[:, :1]
    for h in range(parts):
        load(h).wait()
        spot = slice(h * part, (h + 1) * part)
        own[spot, :] = whiten(traces_ref[spot, :], alive[spot])
        if h == 0:
            peers = (z > 0).astype(jnp.int32) + (z < deep - 1).astype(jnp.int32)
            pl.semaphore_wait(barrier, peers + (wide - 1 + across - 1))
        send_own(h, start)
    keep_col = pltpu.make_async_copy(own, col_ref.at[row], local_sem.at[0])
    keep_row = pltpu.make_async_copy(own, row_ref.at[col], local_sem.at[1])
    keep_col.start()
    keep_row.start()

    for hop in range(1, deep):
        for h in range(parts):
            @pl.when(z + hop < deep)
            def _(hop=hop, h=h):
                arrived(col_ref, row + hop * wide, h, col_recv)
                send_on(hop, h, start)
        if hop == 1:
            for h in range(relayed):
                @pl.when(relays)
                def _(h=h):
                    arrived(col_ref, row + 1, h, col_recv)
                    relay(h, start)

    for step in range(1, wide):
        other = (x + step) % wide
        for h in range(parts):
            due = other > x
            if h < relayed:
                due = due & jnp.logical_not(relays)
            pl.when(due)(
                lambda other=other, h=h: arrived(col_ref, z * wide + other, h, col_recv))
            for hop in range(1, deep):
                pl.when(z + hop < deep)(lambda other=other, hop=hop, h=h: arrived(
                    col_ref, (z + hop) * wide + other, h, col_recv))
    for step in range(1, across):
        for h in range(parts):
            arrived(row_ref, (col + step) % across, h, row_recv)

    keep_col.wait()
    keep_row.wait()
    for h in range(parts):
        send_own(h, sent)
        for hop in range(1, deep):
            pl.when(z + hop < deep)(lambda hop=hop, h=h: send_on(hop, h, sent))
    for h in range(relayed):
        pl.when(relays)(lambda h=h: relay(h, sent))


def gather(traces, alive):
    block, length = traces.shape
    rows, across = lax.axis_size("row"), lax.axis_size("col")
    deep = 4 if rows % 4 == 0 else 1
    wide = rows // deep
    parts = PARTS
    return pl.pallas_call(
        functools.partial(gather_kernel, (deep, wide, across, parts)),
        out_shape=(
            jax.ShapeDtypeStruct((across, block, length), jnp.bfloat16),
            jax.ShapeDtypeStruct((rows, block, length), jnp.bfloat16),
        ),
        in_specs=[pl.BlockSpec(memory_space=pltpu.HBM)] * 2,
        out_specs=(pl.BlockSpec(memory_space=pl.ANY), pl.BlockSpec(memory_space=pl.ANY)),
        scratch_shapes=[
            pltpu.VMEM((block, length), jnp.bfloat16),
            pltpu.VMEM((1, block), jnp.int32),
            pltpu.VMEM((block, length), jnp.bfloat16),
            pltpu.SemaphoreType.DMA((deep, parts)),
            pltpu.SemaphoreType.DMA((deep, wide, parts)),
            pltpu.SemaphoreType.DMA((across, parts)),
            pltpu.SemaphoreType.DMA((parts,)),
            pltpu.SemaphoreType.DMA((rows, parts)),
            pltpu.SemaphoreType.DMA((across, parts)),
            pltpu.SemaphoreType.DMA((2,)),
            pltpu.SemaphoreType.DMA((parts + 1,)),
        ],
        compiler_params=pltpu.CompilerParams(
            collective_id=0, has_side_effects=True, vmem_limit_bytes=16 * 1024 * 1024),
        name="gather",
    )(in_hbm(traces), in_hbm(alive.reshape(1, block)))


def shifted(array, amount):
    width, length = array.shape
    empty = jnp.zeros((width, abs(amount)), array.dtype)
    if amount == 0:
        return array
    if amount > 0:
        return jnp.concatenate([empty, array[:, : length - amount]], axis=1)
    return jnp.concatenate([array[:, -amount:], empty], axis=1)


def pair_kernel(pair_ref, row_ref, col_ref, out_hbm, out_ref, lefts, rights, sems):
    across, width, length = row_ref.shape
    slots = out_ref.shape[0]
    scale = 1.0 / length
    row_first = lax.axis_index("row") * across
    pieces = ((0, REACH), (REACH, LAGS))

    def product(a, b):
        return lax.dot_general(
            a, b, (((1,), (1,)), ((), ())), preferred_element_type=jnp.float32)

    def store(slot, piece):
        spot = pl.ds(pieces[piece][0], pieces[piece][1] - pieces[piece][0])
        return pltpu.make_async_copy(
            out_ref.at[slot, spot], out_hbm.at[slot, spot], sems.at[slot, piece])

    def one_slot(slot, carry):
        first, second = pair_ref[0, slot], pair_ref[1, slot]

        @pl.when(first < 0)
        def _():
            out_ref[slot] = jnp.zeros(out_ref.shape[1:], out_ref.dtype)
            store(slot, 0).start()
            store(slot, 1).start()

        @pl.when(first >= 0)
        def _():
            left = row_ref[jnp.clip(first - row_first, 0, across - 1)]
            right = col_ref[jnp.maximum(second, 0) // across]
            for side, sign in enumerate((-1, 1)):
                if sign == 1:
                    out_ref[slot, REACH] = (product(left, right) * scale).astype(jnp.bfloat16)
                for shift in range(STEP):
                    lefts[side, shift * width : (shift + 1) * width, :] = shifted(
                        left, sign * (shift + 1))
                for pair in range(REACH // STEP // 2):
                    for half in range(2):
                        rights[side, pair, half * width : (half + 1) * width, :] = shifted(
                            right, -sign * STEP * (2 * pair + half))
                    summed = product(lefts[side], rights[side, pair])
                    scaled = (summed * scale).astype(jnp.bfloat16)
                    for half in range(2):
                        for shift in range(STEP):
                            lag = REACH + sign * (STEP * (2 * pair + half) + shift + 1)
                            out_ref[slot, lag] = scaled[
                                shift * width : (shift + 1) * width,
                                half * width : (half + 1) * width]
                store(slot, side).start()

        return carry

    lax.fori_loop(0, slots, one_slot, 0)

    def finish(slot, carry):
        store(slot, 0).wait()
        store(slot, 1).wait()
        return carry

    lax.fori_loop(0, slots, finish, 0)


def correlate(pair_list, row_panel, col_panel):
    slots = pair_list.shape[0]
    _, width, length = row_panel.shape
    return pl.pallas_call(
        pair_kernel,
        in_specs=[
            pl.BlockSpec(memory_space=pltpu.SMEM),
            pl.BlockSpec(memory_space=pltpu.VMEM),
            pl.BlockSpec(memory_space=pltpu.VMEM),
        ],
        out_specs=pl.BlockSpec(memory_space=pltpu.HBM),
        out_shape=jax.ShapeDtypeStruct((slots, LAGS, width, width), jnp.bfloat16),
        scratch_shapes=[
            pltpu.VMEM((slots, LAGS, width, width), jnp.bfloat16),
            pltpu.VMEM((2, STEP * width, length), jnp.bfloat16),
            pltpu.VMEM((2, REACH // STEP // 2, 2 * width, length), jnp.bfloat16),
            pltpu.SemaphoreType.DMA((slots, 2)),
        ],
        compiler_params=pltpu.CompilerParams(vmem_limit_bytes=40 * 1024 * 1024),
        name="pairs",
    )(in_hbm(pair_list.T), row_panel, col_panel)


def shards(traces, alive, pair_list):
    row_panel, col_panel = gather(traces, alive)
    lagged = correlate(pair_list, row_panel, col_panel)
    return jnp.transpose(lagged, (0, 2, 1, 3))


def solution(mesh):
    in_specs = (P(("row", "col"), None), P(("row", "col")), P(("row", "col"), None))
    out_specs = P(("row", "col"), None, None, None)
    return jax.shard_map(shards, mesh=mesh, in_specs=in_specs, out_specs=out_specs, check_vma=False)
```

time: 252 us -> 40.6 us (0.16)
  local copies, waits for them, and re-layouts: 106 us -> 0 us
  waiting for transfers between devices: 69 us -> 0 us
  matrix products: 46.1 us -> 0 us
  Pallas kernels: 0 us -> 40.4 us
  between operations: 13.4 us -> 0.01 us
  loops' own time: 9.85 us -> 0 us
  other arithmetic: 6.78 us -> 0 us
    all_gather x2 -> x0, waiting for transfers between devices: 68.3 us -> none  [the longest x1 51.4 us: shards(): col_panel = lax.all_gather(whitened, 'row', axis=0, tiled=True)]
    while x264 -> x0, local copies, waits for them, and re-layouts: 61.9 us -> none
    dot_general x4 -> x0, matrix products: 46.1 us -> none  [correlate(): lax.dot_general(left_block, shifted, (((1,), (1,)), ((), ())), preferred_...]
    pallas_call x0 -> x2, Pallas kernels: none -> 40.4 us  [the longest x1 28.4 us: gather(): pl.pallas_call(functools.partial(gather_kernel, (deep, wide, across, part...]
    dynamic_update_slice x8 -> x0, local copies, waits for them, and re-layouts: 19.1 us -> none  [one_slot(): lax.dynamic_update_index_in_dim(result, correlate(left_of(slot), right_bl...]
    another operation x1 -> x0, loops' own time: 9.85 us -> none  [shards(): correlations = lax.fori_loop(0, living, one_slot, buffer)]
    convert_element_type x4 -> x0, local copies, waits for them, and re-layouts: 9.8 us -> none  [correlate(): (summed * (1.0 / length)).reshape(width, LAGS, width).astype(jnp.bfloat16)]
    dynamic_slice x12 -> x0, local copies, waits for them, and re-layouts: 8.87 us -> none  [the longest x4 3.89 us: one_slot(): lax.dynamic_slice_in_dim(col_panel, col_place[slot] * block, block, 0)]
  transfers between devices with their start and end apart: 2 -> 0, of which waited for: 2 -> 0; matrix products, arithmetic and copies ran while one was open for 1% -> 0% of each run, Pallas kernels for 0% -> 0%
where the time goes in v2:
time: 40.6 us; the launch traced here: 40.4 us
  Pallas kernels  40.4 us (100%)
    pallas_call x1, Pallas kernels, gather(): pl.pallas_call(functools.partial(gather_kernel, (deep, wide, across, part...  28.4 us
    pallas_call x1, Pallas kernels, correlate(): pl.pallas_call(pair_kernel, in_specs=[pl.BlockSpec(memory_space=pltpu.SME...  12.1 us

profile of v2, /device:TPU:0, one launch (start us, length us, event | category | flops | bytes accessed | tf_op | source)
XLA Modules:
  0.0 40.4 jit_solution(3170718246841502886)
XLA Ops:
  0.0 28.4 %gather.1 = (bf16[4,128,1024]{2,1,0:T(8,128)(2,1)S(1)}, bf16[8,128,1024]{2,1,0:T(8,128)(2,1)S(1)}) custom-call(bf16[128,1024]{1,0:T(8,128)(2,1)} %traces_hbm.1, s32[1,128]{1,0:T(1,128)} %bitcast.4), custom_call_target="tpu_custom_call" | custom-call | tf_op jit(solution)/shard_map/gather/pallas_call | solution.py:169
  28.4 12.1 %pairs.1 = bf16[4,65,128,128]{3,2,1,0:T(8,128)(2,1)} custom-call(s32[2,4]{1,0:T(2,128)} %bitcast.3, bf16[4,128,1024]{2,1,0:T(8,128)(2,1)S(1)} %get-tuple-element.7.row_ref, bf16[8,128,1024]{2,1,0:T(8,128)(2,1)S(1)} %get-tuple-element.8.col_ref), custom_call_target="tpu_custom_call" | custom-call | tf_op jit(solution)/shard_map/pairs/pallas_call | solution.py:270

commit v3 on v2

--- a/solution.py
+++ b/solution.py
@@ -34,7 +34,6 @@
     part = own.shape[0] // parts
     relayed = parts // 2 if wide == 2 and deep > 1 else 0
     relays = (z == 1) & (x == 0)
-    spared = (z == 0) & (x == 1)
 
     load_alive = pltpu.make_async_copy(alive_hbm, alive_ref, load_sem.at[parts])
     load_alive.start()
@@ -82,22 +81,31 @@
         spot = ref.at[place, piece(h)]
         pltpu.make_async_copy(spot, spot, sem.at[place, h]).wait()
 
-    def send_own(h, verb):
-        pl.when(z > 0)(lambda: verb(down(own, row, h, z_send.at[z, h])))
+    def pass_down(hop, h, verb):
+        block = row + hop * wide
+        source = col_ref.at[block] if hop else own
+        pl.when((z > 0) & (z + hop < deep))(
+            lambda: verb(down(source, block, h, z_send.at[z + hop, h])))
+
+    def pass_aside(hop, h, verb):
+        block = row + hop * wide
         for step in range(1, wide):
-            pl.when((x + step) % wide < x)(lambda step=step: verb(side(own, row, step, h)))
+            if hop == 0:
+                due = (x + step) % wide < x
+            elif hop == 1 and h < relayed:
+                due = (z + hop < deep) & ((z != 0) | (x != 1))
+            else:
+                due = z + hop < deep
+            source = col_ref.at[block] if hop else own
+            pl.when(due)(lambda step=step: verb(side(source, block, step, h)))
+
+    def pass_along(h, verb):
         for step in range(1, across):
             verb(along(step, h))
 
-    def send_on(hop, h, verb):
-        block = row + hop * wide
-        pl.when(z > 0)(lambda: verb(down(col_ref.at[block], block, h, z_send.at[z + hop, h])))
-        for step in range(1, wide):
-            go = lambda step=step: verb(side(col_ref.at[block], block, step, h))
-            if hop == 1 and h < relayed:
-                pl.when(jnp.logical_not(spared))(go)
-            else:
-                go()
+    def pass_on(hop, h):
+        pass_down(hop, h, start)
+        pass_aside(hop, h, start)
 
     def relay(h, verb):
         block = row + 1
@@ -116,7 +124,8 @@
         if h == 0:
             peers = (z > 0).astype(jnp.int32) + (z < deep - 1).astype(jnp.int32)
             pl.semaphore_wait(barrier, peers + (wide - 1 + across - 1))
-        send_own(h, start)
+        pass_on(0, h)
+        pass_along(h, start)
     keep_col = pltpu.make_async_copy(own, col_ref.at[row], local_sem.at[0])
     keep_row = pltpu.make_async_copy(own, row_ref.at[col], local_sem.at[1])
     keep_col.start()
@@ -124,16 +133,14 @@
 
     for hop in range(1, deep):
         for h in range(parts):
-            @pl.when(z + hop < deep)
-            def _(hop=hop, h=h):
-                arrived(col_ref, row + hop * wide, h, col_recv)
-                send_on(hop, h, start)
-        if hop == 1:
-            for h in range(relayed):
-                @pl.when(relays)
-                def _(h=h):
-                    arrived(col_ref, row + 1, h, col_recv)
-                    relay(h, start)
+            pl.when(z + hop < deep)(
+                lambda hop=hop, h=h: arrived(col_ref, row + hop * wide, h, col_recv))
+            pass_on(hop, h)
+    for h in range(relayed):
+        @pl.when(relays)
+        def _(h=h):
+            arrived(col_ref, row + 1, h, col_recv)
+            relay(h, start)
 
     for step in range(1, wide):
         other = (x + step) % wide
@@ -153,9 +160,11 @@
     keep_col.wait()
     keep_row.wait()
     for h in range(parts):
-        send_own(h, sent)
-        for hop in range(1, deep):
-            pl.when(z + hop < deep)(lambda hop=hop, h=h: send_on(hop, h, sent))
+        pass_along(h, sent)
+    for hop in range(deep):
+        for h in range(parts):
+            pass_down(hop, h, sent)
+            pass_aside(hop, h, sent)
     for h in range(relayed):
         pl.when(relays)(lambda h=h: relay(h, sent))
 
@@ -225,8 +234,8 @@
         @pl.when(first < 0)
         def _():
             out_ref[slot] = jnp.zeros(out_ref.shape[1:], out_ref.dtype)
-            store(slot, 0).start()
-            store(slot, 1).start()
+            for piece in range(len(pieces)):
+                store(slot, piece).start()
 
         @pl.when(first >= 0)
         def _():
@@ -257,8 +266,8 @@
     lax.fori_loop(0, slots, one_slot, 0)
 
     def finish(slot, carry):
-        store(slot, 0).wait()
-        store(slot, 1).wait()
+        for piece in range(len(pieces)):
+            store(slot, piece).wait()
         return carry
 
     lax.fori_loop(0, slots, finish, 0)

time: 40.6 us -> 39.8 us (0.980)
  Pallas kernels: 40.4 us -> 39.6 us
    pallas_call x1, Pallas kernels: 28.4 us -> 27.6 us  [gather(): pl.pallas_call(functools.partial(gather_kernel, (deep, wide, across, part...]
where the time goes in v3:
time: 39.8 us; the launch traced here: 39.7 us
  Pallas kernels  39.6 us (99%)
    pallas_call x1, Pallas kernels, gather(): pl.pallas_call(functools.partial(gather_kernel, (deep, wide, across, part...  27.6 us
    pallas_call x1, Pallas kernels, correlate(): pl.pallas_call(pair_kernel, in_specs=[pl.BlockSpec(memory_space=pltpu.SME...  12.1 us

profile of v3, /device:TPU:0, one launch (start us, length us, event | category | flops | bytes accessed | tf_op | source)
XLA Modules:
  0.0 39.7 jit_solution(3875531601227777589)
XLA Ops:
  0.0 27.6 %gather.1 = (bf16[4,128,1024]{2,1,0:T(8,128)(2,1)S(1)}, bf16[8,128,1024]{2,1,0:T(8,128)(2,1)S(1)}) custom-call(bf16[128,1024]{1,0:T(8,128)(2,1)} %traces_hbm.1, s32[1,128]{1,0:T(1,128)} %bitcast.4), custom_call_target="tpu_custom_call" | custom-call | tf_op jit(solution)/shard_map/gather/pallas_call | solution.py:178
  27.6 12.1 %pairs.1 = bf16[4,65,128,128]{3,2,1,0:T(8,128)(2,1)} custom-call(s32[2,4]{1,0:T(2,128)} %bitcast.3, bf16[4,128,1024]{2,1,0:T(8,128)(2,1)S(1)} %get-tuple-element.7.row_ref, bf16[8,128,1024]{2,1,0:T(8,128)(2,1)S(1)} %get-tuple-element.8.col_ref), custom_call_target="tpu_custom_call" | custom-call | tf_op jit(solution)/shard_map/pairs/pallas_call | solution.py:279
